TPU v7x, 128 devices: a whole 4x4x4 slice. The times are simulated.
128 devices in a mesh: leaf: 4 (over y), dp: 32 (over z, x, core).
Axes of the slice: x: 4, y: 4, z: 4, core: 2. Of those that a mesh axis runs over, the one named last changes fastest.
Arguments:
- bins: int32 [49152, 256], P('dp'), may hold values from 0 to 255
- outcome: float32 [49152], P('dp'), may hold values from -6 to 6
- treatment: int32 [49152], P('dp'), may hold values 0 or 1
- bag: int32 [196608], P(('leaf', 'dp')), parts along dimension 0, may hold values 0 or 1
- block_node: int32 [384], P('dp'), may hold values from 0 to 15, as said below
Outputs:
- hist_sum: float32 [1024, 16, 256], P(('leaf', 'dp')), parts along dimension 0
- hist_count: float32 [1024, 16, 256], P(('leaf', 'dp')), parts along dimension 0
There are 4 independent parts, one for each index of `leaf`. A program takes and returns all parts, laid end to end along the dimension named above; an argument that names none is the same for every part. Nothing has to cross between parts.
Inputs may be any that keep to these rules, and one draw needn't show every extreme that they name: block_node is nondecreasing along the blocks; every node has 1 to 128 blocks, one exactly that many.
All inputs are finite; a program needn't handle non-finite values. No bound on the sum of `treatment` or of `bag` on one device may be relied on, other than what follows from the above.
Results may differ from a plain program's by a relative error of at most 0.0029.
Values may be sent and summed in bfloat16 or wider, within the bound.
No kernel may reach another device: no remote copies, remote signals or barrier semaphores. Data moves between devices by JAX's collectives and lax.ppermute only.
A program may use at most 64 MiB of HBM per device.

v0:
```python
import math
import jax
import jax.numpy as jnp
from jax import lax
from jax.sharding import PartitionSpec as P

BINS = 256
NODES = 16


def node_params(moments):
    count_n = moments[:, 0]
    sum_w = moments[:, 1]
    sum_y = moments[:, 2]
    sum_wy = moments[:, 3]
    shrunk = count_n + 1.0
    wbar = sum_w / shrunk
    ybar = sum_y / shrunk
    cov = sum_wy - wbar * sum_y - ybar * sum_w + count_n * wbar * ybar
    spread = sum_w - 2.0 * wbar * sum_w + count_n * wbar * wbar + 1.0
    effect = cov / spread
    return jnp.stack([wbar, ybar, effect, shrunk / spread], 1)


def histogram_term(bins, left, count):
    row_count = bins.shape[0]
    width = left.shape[1]
    group = math.gcd(count, 16)
    grouped = bins.reshape(row_count, count // group, group).transpose(1, 0, 2)

    def one_group(picked):
        table = (picked[:, :, None] == jnp.arange(BINS, dtype=jnp.int32)[None, None, :]).astype(
            jnp.bfloat16
        )
        return jnp.einsum("rm,rgb->gmb", left, table, preferred_element_type=jnp.float32)

    return lax.map(one_group, grouped).reshape(count, width, BINS)


def shards(bins, outcome, treatment, bag, block_node):
    row_count = bins.shape[0]
    block_count = block_node.shape[0]
    per_block = row_count // block_count
    own_features = bins.shape[1] // lax.axis_size("dp")
    block_hot = (block_node[:, None] == jnp.arange(NODES, dtype=jnp.int32)[None, :]).astype(
        jnp.float32
    )
    weight = treatment.astype(jnp.float32)
    taken = bag.astype(jnp.float32)
    taken_low = taken.astype(jnp.bfloat16)
    stats = jnp.stack([taken, taken * weight, taken * outcome, taken * weight * outcome], 1)
    block_stats = stats.reshape(block_count, per_block, 4).sum(axis=1)
    local_moments = jnp.dot(block_hot.T, block_stats, precision=lax.Precision.HIGHEST)
    row_hot = jnp.repeat(block_hot, per_block, axis=0).astype(jnp.bfloat16)
    count_left = row_hot * taken_low[:, None]
    moments = lax.psum(local_moments, "dp")
    params = node_params(moments)
    block_params = jnp.dot(block_hot, params, precision=lax.Precision.HIGHEST)
    row_params = jnp.repeat(block_params, per_block, axis=0)
    centred = weight - row_params[:, 0]
    rho = (
        taken
        * centred
        * (outcome - row_params[:, 1] - centred * row_params[:, 2])
        * row_params[:, 3]
    )
    rho_low = rho.astype(jnp.bfloat16)
    sum_left = row_hot * rho_low[:, None]
    both_left = jnp.concatenate([sum_left, count_left], axis=1)
    both = lax.psum_scatter(
        histogram_term(bins, both_left, own_features * lax.axis_size("dp")),
        "dp",
        scatter_dimension=0,
        tiled=True,
    )
    hist_sum = both[:, :NODES]
    hist_count = both[:, NODES:]
    return (hist_sum, hist_count)


def solution(mesh):
    return jax.shard_map(
        shards,
        mesh=mesh,
        in_specs=(P("dp", None), P("dp"), P("dp"), P(("leaf", "dp")), P("dp")),
        out_specs=(P(("leaf", "dp"), None, None), P(("leaf", "dp"), None, None)),
        check_vma=False,
    )
```

profile of v0, /device:TPU:0, one launch (start us, length us, event | category | flops | bytes accessed | tf_op | source)
XLA Modules:
  0.0 305.6 jit_solution(4352091207590178504)
XLA Ops:
  7.2 0.0 reduce-scatter.2.cloned.1.call-start
  7.2 0.7 convert_bitcast_fusion
  7.9 0.7 convert_convert_fusion.1
  8.6 0.7 fusion.9
  9.3 0.1 maximum_reduce_fusion
  9.4 0.8 fusion.6
  10.2 68.4 %psum.7 = f32[16,4]{0,1:T(4,128)S(1)} all-reduce(f32[16,4]{0,1:T(4,128)S(1)} %fusion.6), channel_id=1, replica_groups=mesh['leaf'=4,'dp'=32] {'dp'}, use_global_device_ids=true, to_apply=%region_1.0 | all-reduce | flops 64 | bytes 512 | tf_op jit(solution)/shard_map/psum | solution.py:56
  78.6 0.8 fusion.5
  79.4 0.1 broadcast_bitcast_fusion
  79.5 0.1 slice_reduce_fusion.3
  79.6 1.9 copy.11
  81.5 0.7 multiply_convert_fusion
  82.2 0.1 broadcast_in_dim.20
  82.4 125.3 %while.10 = (s32[]{:T(128)}, f32[16,16,32,256]{3,2,1,0:T(8,128)}, s32[16,1536,16]{1,2,0:T(8,128)S(1)}, bf16[1536,32]{0,1:T(8,128)(2,1)S(1)}, s32[]{:T(128)}) while((s32[]{:T(128)}, f32[16,16,32,256]{3,2,1,0:T(8,128)}, s32[16,1536,16]{1,2,0:T(8,128)S(1)}, bf16[1536,32]{0,1:T(8,128)(2,1)S(1)}, s32[]{:T(128)}) %tuple.37), condition=%wide.region_3.4_spmd, body=%wide.region_2.3_spmd.sunk | while | flops 408944640 | bytes 918081 | solution.py:37
  82.4 7.8 %fusion.28 = f32[16,16,32,256]{3,2,1,0:T(8,128)} fusion(f32[16,16,32,256]{3,2,1,0:T(8,128)} %get-tuple-element.80, s32[]{:T(128)} %get-tuple-element.79, s32[1536,16]{0,1:T(8,128)S(1)} %dynamic-slice_bitcast_fusion.2, bf16[1536,32]{0,1:T(8,128)(2,1)S(1)} %get-tuple-element.87), kind=kOutput, calls=%fused_computation.4.clone.1 | convolution fusion | flops 408944640 | bytes 721408 | tf_op jit(solution)/shard_map/while/body/eval_jaxpr/rm,rgb->gmb/dot_general | solution.py:35
  90.2 7.8 %fusion.28 = f32[16,16,32,256]{3,2,1,0:T(8,128)} fusion(f32[16,16,32,256]{3,2,1,0:T(8,128)} %get-tuple-element.80, s32[]{:T(128)} %get-tuple-element.79, s32[1536,16]{0,1:T(8,128)S(1)} %dynamic-slice_bitcast_fusion.2, bf16[1536,32]{0,1:T(8,128)(2,1)S(1)} %get-tuple-element.87), kind=kOutput, calls=%fused_computation.4.clone.1 | convolution fusion | flops 408944640 | bytes 721408 | tf_op jit(solution)/shard_map/while/body/eval_jaxpr/rm,rgb->gmb/dot_general | solution.py:35
  98.1 7.8 %fusion.28 = f32[16,16,32,256]{3,2,1,0:T(8,128)} fusion(f32[16,16,32,256]{3,2,1,0:T(8,128)} %get-tuple-element.80, s32[]{:T(128)} %get-tuple-element.79, s32[1536,16]{0,1:T(8,128)S(1)} %dynamic-slice_bitcast_fusion.2, bf16[1536,32]{0,1:T(8,128)(2,1)S(1)} %get-tuple-element.87), kind=kOutput, calls=%fused_computation.4.clone.1 | convolution fusion | flops 408944640 | bytes 721408 | tf_op jit(solution)/shard_map/while/body/eval_jaxpr/rm,rgb->gmb/dot_general | solution.py:35
  105.9 7.8 %fusion.28 = f32[16,16,32,256]{3,2,1,0:T(8,128)} fusion(f32[16,16,32,256]{3,2,1,0:T(8,128)} %get-tuple-element.80, s32[]{:T(128)} %get-tuple-element.79, s32[1536,16]{0,1:T(8,128)S(1)} %dynamic-slice_bitcast_fusion.2, bf16[1536,32]{0,1:T(8,128)(2,1)S(1)} %get-tuple-element.87), kind=kOutput, calls=%fused_computation.4.clone.1 | convolution fusion | flops 408944640 | bytes 721408 | tf_op jit(solution)/shard_map/while/body/eval_jaxpr/rm,rgb->gmb/dot_general | solution.py:35
  113.7 7.8 %fusion.28 = f32[16,16,32,256]{3,2,1,0:T(8,128)} fusion(f32[16,16,32,256]{3,2,1,0:T(8,128)} %get-tuple-element.80, s32[]{:T(128)} %get-tuple-element.79, s32[1536,16]{0,1:T(8,128)S(1)} %dynamic-slice_bitcast_fusion.2, bf16[1536,32]{0,1:T(8,128)(2,1)S(1)} %get-tuple-element.87), kind=kOutput, calls=%fused_computation.4.clone.1 | convolution fusion | flops 408944640 | bytes 721408 | tf_op jit(solution)/shard_map/while/body/eval_jaxpr/rm,rgb->gmb/dot_general | solution.py:35
  121.6 7.8 %fusion.28 = f32[16,16,32,256]{3,2,1,0:T(8,128)} fusion(f32[16,16,32,256]{3,2,1,0:T(8,128)} %get-tuple-element.80, s32[]{:T(128)} %get-tuple-element.79, s32[1536,16]{0,1:T(8,128)S(1)} %dynamic-slice_bitcast_fusion.2, bf16[1536,32]{0,1:T(8,128)(2,1)S(1)} %get-tuple-element.87), kind=kOutput, calls=%fused_computation.4.clone.1 | convolution fusion | flops 408944640 | bytes 721408 | tf_op jit(solution)/shard_map/while/body/eval_jaxpr/rm,rgb->gmb/dot_general | solution.py:35
  129.4 7.8 %fusion.28 = f32[16,16,32,256]{3,2,1,0:T(8,128)} fusion(f32[16,16,32,256]{3,2,1,0:T(8,128)} %get-tuple-element.80, s32[]{:T(128)} %get-tuple-element.79, s32[1536,16]{0,1:T(8,128)S(1)} %dynamic-slice_bitcast_fusion.2, bf16[1536,32]{0,1:T(8,128)(2,1)S(1)} %get-tuple-element.87), kind=kOutput, calls=%fused_computation.4.clone.1 | convolution fusion | flops 408944640 | bytes 721408 | tf_op jit(solution)/shard_map/while/body/eval_jaxpr/rm,rgb->gmb/dot_general | solution.py:35
  137.2 7.8 %fusion.28 = f32[16,16,32,256]{3,2,1,0:T(8,128)} fusion(f32[16,16,32,256]{3,2,1,0:T(8,128)} %get-tuple-element.80, s32[]{:T(128)} %get-tuple-element.79, s32[1536,16]{0,1:T(8,128)S(1)} %dynamic-slice_bitcast_fusion.2, bf16[1536,32]{0,1:T(8,128)(2,1)S(1)} %get-tuple-element.87), kind=kOutput, calls=%fused_computation.4.clone.1 | convolution fusion | flops 408944640 | bytes 721408 | tf_op jit(solution)/shard_map/while/body/eval_jaxpr/rm,rgb->gmb/dot_general | solution.py:35
  145.1 7.8 %fusion.28 = f32[16,16,32,256]{3,2,1,0:T(8,128)} fusion(f32[16,16,32,256]{3,2,1,0:T(8,128)} %get-tuple-element.80, s32[]{:T(128)} %get-tuple-element.79, s32[1536,16]{0,1:T(8,128)S(1)} %dynamic-slice_bitcast_fusion.2, bf16[1536,32]{0,1:T(8,128)(2,1)S(1)} %get-tuple-element.87), kind=kOutput, calls=%fused_computation.4.clone.1 | convolution fusion | flops 408944640 | bytes 721408 | tf_op jit(solution)/shard_map/while/body/eval_jaxpr/rm,rgb->gmb/dot_general | solution.py:35
  152.9 7.8 %fusion.28 = f32[16,16,32,256]{3,2,1,0:T(8,128)} fusion(f32[16,16,32,256]{3,2,1,0:T(8,128)} %get-tuple-element.80, s32[]{:T(128)} %get-tuple-element.79, s32[1536,16]{0,1:T(8,128)S(1)} %dynamic-slice_bitcast_fusion.2, bf16[1536,32]{0,1:T(8,128)(2,1)S(1)} %get-tuple-element.87), kind=kOutput, calls=%fused_computation.4.clone.1 | convolution fusion | flops 408944640 | bytes 721408 | tf_op jit(solution)/shard_map/while/body/eval_jaxpr/rm,rgb->gmb/dot_general | solution.py:35
  160.7 7.8 %fusion.28 = f32[16,16,32,256]{3,2,1,0:T(8,128)} fusion(f32[16,16,32,256]{3,2,1,0:T(8,128)} %get-tuple-element.80, s32[]{:T(128)} %get-tuple-element.79, s32[1536,16]{0,1:T(8,128)S(1)} %dynamic-slice_bitcast_fusion.2, bf16[1536,32]{0,1:T(8,128)(2,1)S(1)} %get-tuple-element.87), kind=kOutput, calls=%fused_computation.4.clone.1 | convolution fusion | flops 408944640 | bytes 721408 | tf_op jit(solution)/shard_map/while/body/eval_jaxpr/rm,rgb->gmb/dot_general | solution.py:35
  168.5 7.8 %fusion.28 = f32[16,16,32,256]{3,2,1,0:T(8,128)} fusion(f32[16,16,32,256]{3,2,1,0:T(8,128)} %get-tuple-element.80, s32[]{:T(128)} %get-tuple-element.79, s32[1536,16]{0,1:T(8,128)S(1)} %dynamic-slice_bitcast_fusion.2, bf16[1536,32]{0,1:T(8,128)(2,1)S(1)} %get-tuple-element.87), kind=kOutput, calls=%fused_computation.4.clone.1 | convolution fusion | flops 408944640 | bytes 721408 | tf_op jit(solution)/shard_map/while/body/eval_jaxpr/rm,rgb->gmb/dot_general | solution.py:35
  176.4 7.8 %fusion.28 = f32[16,16,32,256]{3,2,1,0:T(8,128)} fusion(f32[16,16,32,256]{3,2,1,0:T(8,128)} %get-tuple-element.80, s32[]{:T(128)} %get-tuple-element.79, s32[1536,16]{0,1:T(8,128)S(1)} %dynamic-slice_bitcast_fusion.2, bf16[1536,32]{0,1:T(8,128)(2,1)S(1)} %get-tuple-element.87), kind=kOutput, calls=%fused_computation.4.clone.1 | convolution fusion | flops 408944640 | bytes 721408 | tf_op jit(solution)/shard_map/while/body/eval_jaxpr/rm,rgb->gmb/dot_general | solution.py:35
  184.2 7.8 %fusion.28 = f32[16,16,32,256]{3,2,1,0:T(8,128)} fusion(f32[16,16,32,256]{3,2,1,0:T(8,128)} %get-tuple-element.80, s32[]{:T(128)} %get-tuple-element.79, s32[1536,16]{0,1:T(8,128)S(1)} %dynamic-slice_bitcast_fusion.2, bf16[1536,32]{0,1:T(8,128)(2,1)S(1)} %get-tuple-element.87), kind=kOutput, calls=%fused_computation.4.clone.1 | convolution fusion | flops 408944640 | bytes 721408 | tf_op jit(solution)/shard_map/while/body/eval_jaxpr/rm,rgb->gmb/dot_general | solution.py:35
  192.0 7.8 %fusion.28 = f32[16,16,32,256]{3,2,1,0:T(8,128)} fusion(f32[16,16,32,256]{3,2,1,0:T(8,128)} %get-tuple-element.80, s32[]{:T(128)} %get-tuple-element.79, s32[1536,16]{0,1:T(8,128)S(1)} %dynamic-slice_bitcast_fusion.2, bf16[1536,32]{0,1:T(8,128)(2,1)S(1)} %get-tuple-element.87), kind=kOutput, calls=%fused_computation.4.clone.1 | convolution fusion | flops 408944640 | bytes 721408 | tf_op jit(solution)/shard_map/while/body/eval_jaxpr/rm,rgb->gmb/dot_general | solution.py:35
  199.9 7.8 %fusion.28 = f32[16,16,32,256]{3,2,1,0:T(8,128)} fusion(f32[16,16,32,256]{3,2,1,0:T(8,128)} %get-tuple-element.80, s32[]{:T(128)} %get-tuple-element.79, s32[1536,16]{0,1:T(8,128)S(1)} %dynamic-slice_bitcast_fusion.2, bf16[1536,32]{0,1:T(8,128)(2,1)S(1)} %get-tuple-element.87), kind=kOutput, calls=%fused_computation.4.clone.1 | convolution fusion | flops 408944640 | bytes 721408 | tf_op jit(solution)/shard_map/while/body/eval_jaxpr/rm,rgb->gmb/dot_general | solution.py:35
  207.7 89.4 %reduce-scatter.2.cloned.1.call-done = f32[8,32,256]{2,1,0:T(8,128)} async-done(((f32[256,32,256]{2,1,0:T(8,128)}), f32[8,32,256]{2,1,0:T(8,128)}) %reduce-scatter.2.cloned.1.call-update) | async-done | bytes 262160 | tf_op jit(solution)/shard_map/reduce_scatter | solution.py:70
  297.1 1.7 fusion.23
  (23 shorter events, 0.2 us)
Async XLA Ops:
  7.2 289.9 %reduce-scatter.2.cloned.1.call-start = ((), (), s32[]{:S(2)}) async-start(), calls=%async_computation.1 | async-start | bytes 8650752 | tf_op jit(solution)/shard_map/reduce_scatter | solution.py:70
Sparse Core Ops, SparseCore 0:
  207.8 89.1 reduce-scatter.1
where the time goes:
time: 306 us
  matrix products  127 us (42%)
  waiting for transfers between devices  89.4 us (29%)
  blocking collectives  68.4 us (22%)
  between operations  14.1 us (5%)
  local copies, waits for them, and re-layouts  3.94 us (1%)
    dot_general x16, matrix products, one_group(): jnp.einsum('rm,rgb->gmb', left, table, preferred_element_type=jnp.float32)  125 us
    reduce_scatter x1, waiting for transfers between devices, shards(): lax.psum_scatter(histogram_term(bins, both_left, own_features * lax.axis_...  89.4 us
    psum x1, blocking collectives, shards(): moments = lax.psum(local_moments, 'dp')  68.4 us
  transfers between devices with their start and end apart: 1, of which 1 were waited for; matrix products, arithmetic and copies ran while one was open for 0% of the time, Pallas kernels for 0%

commit v1 on v0

--- a/solution.py
+++ b/solution.py
@@ -53,7 +53,11 @@
     local_moments = jnp.dot(block_hot.T, block_stats, precision=lax.Precision.HIGHEST)
     row_hot = jnp.repeat(block_hot, per_block, axis=0).astype(jnp.bfloat16)
     count_left = row_hot * taken_low[:, None]
-    moments = lax.psum(local_moments, "dp")
+    devices = lax.axis_size("dp")
+    moments, far = (local_moments, 1)
+    while far < devices:
+        moments = moments + lax.ppermute(moments, "dp", [(i, i ^ far) for i in range(devices)])
+        far = 2 * far
     params = node_params(moments)
     block_params = jnp.dot(block_hot, params, precision=lax.Precision.HIGHEST)
     row_params = jnp.repeat(block_params, per_block, axis=0)

time: 306 us -> 260 us (0.85)
  blocking collectives: 68.4 us -> 0 us
  waiting for transfers between devices: 89.4 us -> 101 us
  starting transfers between devices: 0.04 us -> 10.7 us
    psum x1 -> x0, blocking collectives: 68.4 us -> none  [shards(): moments = lax.psum(local_moments, 'dp')]
    ppermute x0 -> x5, starting transfers between devices: none -> 10.6 us  [shards(): lax.ppermute(moments, 'dp', [(i, i ^ far) for i in range(devices)])]
    ppermute x0 -> x5, waiting for transfers between devices: none -> 6.07 us  [shards(): lax.ppermute(moments, 'dp', [(i, i ^ far) for i in range(devices)])]
    reduce_scatter x1, waiting for transfers between devices: 89.4 us -> 94.6 us  [shards(): lax.psum_scatter(histogram_term(bins, both_left, own_features * lax.axis_...]
  transfers between devices with their start and end apart: 1 -> 6, of which waited for: 1 -> 5; matrix products, arithmetic and copies ran while one was open for 0% -> 1% of each run, Pallas kernels for 0% -> 0%
where the time goes in v1:
time: 260 us; the launch traced here: 259 us
  matrix products  127 us (49%)
  waiting for transfers between devices  101 us (39%)
  between operations  14.1 us (5%)
  starting transfers between devices  10.7 us (4%)
  local copies, waits for them, and re-layouts  3.94 us (2%)
  other arithmetic  3 us (1%)
    dot_general x16, matrix products, one_group(): jnp.einsum('rm,rgb->gmb', left, table, preferred_element_type=jnp.float32)  125 us
    reduce_scatter x1, waiting for transfers between devices, shards(): lax.psum_scatter(histogram_term(bins, both_left, own_features * lax.axis_...  94.6 us
    ppermute x5, starting transfers between devices, shards(): lax.ppermute(moments, 'dp', [(i, i ^ far) for i in range(devices)])  10.6 us
    ppermute x5, waiting for transfers between devices, shards(): lax.ppermute(moments, 'dp', [(i, i ^ far) for i in range(devices)])  6.07 us
  transfers between devices with their start and end apart: 6, of which 5 were waited for; matrix products, arithmetic and copies ran while one was open for 1% of the time, Pallas kernels for 0%

profile of v1, /device:TPU:0, one launch (start us, length us, event | category | flops | bytes accessed | tf_op | source)
XLA Modules:
  0.0 259.2 jit_solution(12511162113011069848)
XLA Ops:
  7.9 0.7 fusion.9
  8.7 0.8 fusion.6
  9.5 1.2 collective-permute-done
  10.7 1.6 collective-permute-start.1
  12.2 2.0 collective-permute-done.1
  14.3 3.1 %collective-permute-start.2 = (f32[16,4]{0,1:T(4,128)S(1)}, f32[16,4]{0,1:T(4,128)S(1)}, u32[]{:S(2)}, u32[]{:S(2)}) collective-permute-start(f32[16,4]{0,1:T(4,128)S(1)} %add.42), channel_id=1, source_target_pairs={{0,4},{1,5},{2,6},{3,7},{4,0},{5,1},{6,2},{7,3},{8,12},{9,13},{10,... | collective-permute-start | bytes 776 | tf_op jit(solution)/shard_map/ppermute | solution.py:59
  17.4 2.0 collective-permute-done.2
  19.4 2.0 collective-permute-start.3
  22.0 0.9 collective-permute-done.3
  22.9 4.0 %collective-permute-start.4 = (f32[16,4]{0,1:T(4,128)S(1)}, f32[16,4]{0,1:T(4,128)S(1)}, u32[]{:S(2)}, u32[]{:S(2)}) collective-permute-start(f32[16,4]{0,1:T(4,128)S(1)} %add.44), channel_id=1, source_target_pairs={{0,16},{1,17},{2,18},{3,19},{4,20},{5,21},{6,22},{7,23},{8,24},{9,... | collective-permute-start | bytes 776 | tf_op jit(solution)/shard_map/ppermute | solution.py:59
  26.9 1.9 copy.11
  28.8 0.8 fusion.5
  29.8 0.7 multiply_convert_fusion
  30.7 125.3 %while.10 = (s32[]{:T(128)}, f32[16,16,32,256]{3,2,1,0:T(8,128)}, s32[16,1536,16]{1,2,0:T(8,128)S(1)}, bf16[1536,32]{0,1:T(8,128)(2,1)S(1)}, s32[]{:T(128)}) while((s32[]{:T(128)}, f32[16,16,32,256]{3,2,1,0:T(8,128)}, s32[16,1536,16]{1,2,0:T(8,128)S(1)}, bf16[1536,32]{0,1:T(8,128)(2,1)S(1)}, s32[]{:T(128)}) %tuple.37), condition=%wide.region_2.3_spmd, body=%wide.region_1.2_spmd.sunk | while | flops 408944640 | bytes 918081 | solution.py:37
  30.7 7.8 %fusion.28 = f32[16,16,32,256]{3,2,1,0:T(8,128)} fusion(f32[16,16,32,256]{3,2,1,0:T(8,128)} %get-tuple-element.80, s32[]{:T(128)} %get-tuple-element.79, s32[1536,16]{0,1:T(8,128)S(1)} %dynamic-slice_bitcast_fusion.2, bf16[1536,32]{0,1:T(8,128)(2,1)S(1)} %get-tuple-element.87), kind=kOutput, calls=%fused_computation.4.clone.1 | convolution fusion | flops 408944640 | bytes 721408 | tf_op jit(solution)/shard_map/while/body/eval_jaxpr/rm,rgb->gmb/dot_general | solution.py:35
  38.6 7.8 %fusion.28 = f32[16,16,32,256]{3,2,1,0:T(8,128)} fusion(f32[16,16,32,256]{3,2,1,0:T(8,128)} %get-tuple-element.80, s32[]{:T(128)} %get-tuple-element.79, s32[1536,16]{0,1:T(8,128)S(1)} %dynamic-slice_bitcast_fusion.2, bf16[1536,32]{0,1:T(8,128)(2,1)S(1)} %get-tuple-element.87), kind=kOutput, calls=%fused_computation.4.clone.1 | convolution fusion | flops 408944640 | bytes 721408 | tf_op jit(solution)/shard_map/while/body/eval_jaxpr/rm,rgb->gmb/dot_general | solution.py:35
  46.4 7.8 %fusion.28 = f32[16,16,32,256]{3,2,1,0:T(8,128)} fusion(f32[16,16,32,256]{3,2,1,0:T(8,128)} %get-tuple-element.80, s32[]{:T(128)} %get-tuple-element.79, s32[1536,16]{0,1:T(8,128)S(1)} %dynamic-slice_bitcast_fusion.2, bf16[1536,32]{0,1:T(8,128)(2,1)S(1)} %get-tuple-element.87), kind=kOutput, calls=%fused_computation.4.clone.1 | convolution fusion | flops 408944640 | bytes 721408 | tf_op jit(solution)/shard_map/while/body/eval_jaxpr/rm,rgb->gmb/dot_general | solution.py:35
  54.2 7.8 %fusion.28 = f32[16,16,32,256]{3,2,1,0:T(8,128)} fusion(f32[16,16,32,256]{3,2,1,0:T(8,128)} %get-tuple-element.80, s32[]{:T(128)} %get-tuple-element.79, s32[1536,16]{0,1:T(8,128)S(1)} %dynamic-slice_bitcast_fusion.2, bf16[1536,32]{0,1:T(8,128)(2,1)S(1)} %get-tuple-element.87), kind=kOutput, calls=%fused_computation.4.clone.1 | convolution fusion | flops 408944640 | bytes 721408 | tf_op jit(solution)/shard_map/while/body/eval_jaxpr/rm,rgb->gmb/dot_general | solution.py:35
  62.1 7.8 %fusion.28 = f32[16,16,32,256]{3,2,1,0:T(8,128)} fusion(f32[16,16,32,256]{3,2,1,0:T(8,128)} %get-tuple-element.80, s32[]{:T(128)} %get-tuple-element.79, s32[1536,16]{0,1:T(8,128)S(1)} %dynamic-slice_bitcast_fusion.2, bf16[1536,32]{0,1:T(8,128)(2,1)S(1)} %get-tuple-element.87), kind=kOutput, calls=%fused_computation.4.clone.1 | convolution fusion | flops 408944640 | bytes 721408 | tf_op jit(solution)/shard_map/while/body/eval_jaxpr/rm,rgb->gmb/dot_general | solution.py:35
  69.9 7.8 %fusion.28 = f32[16,16,32,256]{3,2,1,0:T(8,128)} fusion(f32[16,16,32,256]{3,2,1,0:T(8,128)} %get-tuple-element.80, s32[]{:T(128)} %get-tuple-element.79, s32[1536,16]{0,1:T(8,128)S(1)} %dynamic-slice_bitcast_fusion.2, bf16[1536,32]{0,1:T(8,128)(2,1)S(1)} %get-tuple-element.87), kind=kOutput, calls=%fused_computation.4.clone.1 | convolution fusion | flops 408944640 | bytes 721408 | tf_op jit(solution)/shard_map/while/body/eval_jaxpr/rm,rgb->gmb/dot_general | solution.py:35
  77.7 7.8 %fusion.28 = f32[16,16,32,256]{3,2,1,0:T(8,128)} fusion(f32[16,16,32,256]{3,2,1,0:T(8,128)} %get-tuple-element.80, s32[]{:T(128)} %get-tuple-element.79, s32[1536,16]{0,1:T(8,128)S(1)} %dynamic-slice_bitcast_fusion.2, bf16[1536,32]{0,1:T(8,128)(2,1)S(1)} %get-tuple-element.87), kind=kOutput, calls=%fused_computation.4.clone.1 | convolution fusion | flops 408944640 | bytes 721408 | tf_op jit(solution)/shard_map/while/body/eval_jaxpr/rm,rgb->gmb/dot_general | solution.py:35
  85.6 7.8 %fusion.28 = f32[16,16,32,256]{3,2,1,0:T(8,128)} fusion(f32[16,16,32,256]{3,2,1,0:T(8,128)} %get-tuple-element.80, s32[]{:T(128)} %get-tuple-element.79, s32[1536,16]{0,1:T(8,128)S(1)} %dynamic-slice_bitcast_fusion.2, bf16[1536,32]{0,1:T(8,128)(2,1)S(1)} %get-tuple-element.87), kind=kOutput, calls=%fused_computation.4.clone.1 | convolution fusion | flops 408944640 | bytes 721408 | tf_op jit(solution)/shard_map/while/body/eval_jaxpr/rm,rgb->gmb/dot_general | solution.py:35
  93.4 7.8 %fusion.28 = f32[16,16,32,256]{3,2,1,0:T(8,128)} fusion(f32[16,16,32,256]{3,2,1,0:T(8,128)} %get-tuple-element.80, s32[]{:T(128)} %get-tuple-element.79, s32[1536,16]{0,1:T(8,128)S(1)} %dynamic-slice_bitcast_fusion.2, bf16[1536,32]{0,1:T(8,128)(2,1)S(1)} %get-tuple-element.87), kind=kOutput, calls=%fused_computation.4.clone.1 | convolution fusion | flops 408944640 | bytes 721408 | tf_op jit(solution)/shard_map/while/body/eval_jaxpr/rm,rgb->gmb/dot_general | solution.py:35
  101.2 7.8 %fusion.28 = f32[16,16,32,256]{3,2,1,0:T(8,128)} fusion(f32[16,16,32,256]{3,2,1,0:T(8,128)} %get-tuple-element.80, s32[]{:T(128)} %get-tuple-element.79, s32[1536,16]{0,1:T(8,128)S(1)} %dynamic-slice_bitcast_fusion.2, bf16[1536,32]{0,1:T(8,128)(2,1)S(1)} %get-tuple-element.87), kind=kOutput, calls=%fused_computation.4.clone.1 | convolution fusion | flops 408944640 | bytes 721408 | tf_op jit(solution)/shard_map/while/body/eval_jaxpr/rm,rgb->gmb/dot_general | solution.py:35
  109.0 7.8 %fusion.28 = f32[16,16,32,256]{3,2,1,0:T(8,128)} fusion(f32[16,16,32,256]{3,2,1,0:T(8,128)} %get-tuple-element.80, s32[]{:T(128)} %get-tuple-element.79, s32[1536,16]{0,1:T(8,128)S(1)} %dynamic-slice_bitcast_fusion.2, bf16[1536,32]{0,1:T(8,128)(2,1)S(1)} %get-tuple-element.87), kind=kOutput, calls=%fused_computation.4.clone.1 | convolution fusion | flops 408944640 | bytes 721408 | tf_op jit(solution)/shard_map/while/body/eval_jaxpr/rm,rgb->gmb/dot_general | solution.py:35
  116.9 7.8 %fusion.28 = f32[16,16,32,256]{3,2,1,0:T(8,128)} fusion(f32[16,16,32,256]{3,2,1,0:T(8,128)} %get-tuple-element.80, s32[]{:T(128)} %get-tuple-element.79, s32[1536,16]{0,1:T(8,128)S(1)} %dynamic-slice_bitcast_fusion.2, bf16[1536,32]{0,1:T(8,128)(2,1)S(1)} %get-tuple-element.87), kind=kOutput, calls=%fused_computation.4.clone.1 | convolution fusion | flops 408944640 | bytes 721408 | tf_op jit(solution)/shard_map/while/body/eval_jaxpr/rm,rgb->gmb/dot_general | solution.py:35
  124.7 7.8 %fusion.28 = f32[16,16,32,256]{3,2,1,0:T(8,128)} fusion(f32[16,16,32,256]{3,2,1,0:T(8,128)} %get-tuple-element.80, s32[]{:T(128)} %get-tuple-element.79, s32[1536,16]{0,1:T(8,128)S(1)} %dynamic-slice_bitcast_fusion.2, bf16[1536,32]{0,1:T(8,128)(2,1)S(1)} %get-tuple-element.87), kind=kOutput, calls=%fused_computation.4.clone.1 | convolution fusion | flops 408944640 | bytes 721408 | tf_op jit(solution)/shard_map/while/body/eval_jaxpr/rm,rgb->gmb/dot_general | solution.py:35
  132.5 7.8 %fusion.28 = f32[16,16,32,256]{3,2,1,0:T(8,128)} fusion(f32[16,16,32,256]{3,2,1,0:T(8,128)} %get-tuple-element.80, s32[]{:T(128)} %get-tuple-element.79, s32[1536,16]{0,1:T(8,128)S(1)} %dynamic-slice_bitcast_fusion.2, bf16[1536,32]{0,1:T(8,128)(2,1)S(1)} %get-tuple-element.87), kind=kOutput, calls=%fused_computation.4.clone.1 | convolution fusion | flops 408944640 | bytes 721408 | tf_op jit(solution)/shard_map/while/body/eval_jaxpr/rm,rgb->gmb/dot_general | solution.py:35
  140.4 7.8 %fusion.28 = f32[16,16,32,256]{3,2,1,0:T(8,128)} fusion(f32[16,16,32,256]{3,2,1,0:T(8,128)} %get-tuple-element.80, s32[]{:T(128)} %get-tuple-element.79, s32[1536,16]{0,1:T(8,128)S(1)} %dynamic-slice_bitcast_fusion.2, bf16[1536,32]{0,1:T(8,128)(2,1)S(1)} %get-tuple-element.87), kind=kOutput, calls=%fused_computation.4.clone.1 | convolution fusion | flops 408944640 | bytes 721408 | tf_op jit(solution)/shard_map/while/body/eval_jaxpr/rm,rgb->gmb/dot_general | solution.py:35
  148.2 7.8 %fusion.28 = f32[16,16,32,256]{3,2,1,0:T(8,128)} fusion(f32[16,16,32,256]{3,2,1,0:T(8,128)} %get-tuple-element.80, s32[]{:T(128)} %get-tuple-element.79, s32[1536,16]{0,1:T(8,128)S(1)} %dynamic-slice_bitcast_fusion.2, bf16[1536,32]{0,1:T(8,128)(2,1)S(1)} %get-tuple-element.87), kind=kOutput, calls=%fused_computation.4.clone.1 | convolution fusion | flops 408944640 | bytes 721408 | tf_op jit(solution)/shard_map/while/body/eval_jaxpr/rm,rgb->gmb/dot_general | solution.py:35
  156.1 94.6 %reduce-scatter.2.cloned.1.call-done = f32[8,32,256]{2,1,0:T(8,128)} async-done(((f32[256,32,256]{2,1,0:T(8,128)}), f32[8,32,256]{2,1,0:T(8,128)}) %reduce-scatter.2.cloned.1.call-update) | async-done | bytes 262160 | tf_op jit(solution)/shard_map/reduce_scatter | solution.py:74
  250.7 1.7 fusion.23
  (37 shorter events, 2.0 us)
Async XLA Ops:
  7.2 243.5 %reduce-scatter.2.cloned.1.call-start = ((), (), s32[]{:S(2)}) async-start(), calls=%async_computation.1 | async-start | bytes 8650752 | tf_op jit(solution)/shard_map/reduce_scatter | solution.py:74
  9.5 1.2 collective-permute-start
  10.7 3.6 %collective-permute-start.1 = (f32[16,4]{0,1:T(4,128)S(1)}, f32[16,4]{0,1:T(4,128)S(1)}, u32[]{:S(2)}, u32[]{:S(2)}) collective-permute-start(f32[16,4]{0,1:T(4,128)S(1)} %add.41), channel_id=1, source_target_pairs={{0,2},{1,3},{2,0},{3,1},{4,6},{5,7},{6,4},{7,5},{8,10},{9,11},{10,... | collective-permute-start | bytes 776 | tf_op jit(solution)/shard_map/ppermute | solution.py:59
  14.3 5.1 %collective-permute-start.2 = (f32[16,4]{0,1:T(4,128)S(1)}, f32[16,4]{0,1:T(4,128)S(1)}, u32[]{:S(2)}, u32[]{:S(2)}) collective-permute-start(f32[16,4]{0,1:T(4,128)S(1)} %add.42), channel_id=1, source_target_pairs={{0,4},{1,5},{2,6},{3,7},{4,0},{5,1},{6,2},{7,3},{8,12},{9,13},{10,... | collective-permute-start | bytes 776 | tf_op jit(solution)/shard_map/ppermute | solution.py:59
  19.4 3.6 %collective-permute-start.3 = (f32[16,4]{0,1:T(4,128)S(1)}, f32[16,4]{0,1:T(4,128)S(1)}, u32[]{:S(2)}, u32[]{:S(2)}) collective-permute-start(f32[16,4]{0,1:T(4,128)S(1)} %add.43), channel_id=1, source_target_pairs={{0,8},{1,9},{2,10},{3,11},{4,12},{5,13},{6,14},{7,15},{8,0},{9,1},... | collective-permute-start | bytes 776 | tf_op jit(solution)/shard_map/ppermute | solution.py:59
  22.9 5.8 %collective-permute-start.4 = (f32[16,4]{0,1:T(4,128)S(1)}, f32[16,4]{0,1:T(4,128)S(1)}, u32[]{:S(2)}, u32[]{:S(2)}) collective-permute-start(f32[16,4]{0,1:T(4,128)S(1)} %add.44), channel_id=1, source_target_pairs={{0,16},{1,17},{2,18},{3,19},{4,20},{5,21},{6,22},{7,23},{8,24},{9,... | collective-permute-start | bytes 776 | tf_op jit(solution)/shard_map/ppermute | solution.py:59
Sparse Core Ops, SparseCore 0:
  156.2 94.4 reduce-scatter.1
